TPU v7x, 128 devices: a whole 4x4x4 slice. The times are simulated.
128 devices in a mesh: row: 4 (over x), col: 8 (over z, core), depth: 4 (over y).
Axes of the slice: x: 4, y: 4, z: 4, core: 2. Of those that a mesh axis runs over, the one named last changes fastest.
Arguments:
- x_in: bfloat16 [4096, 4096], P('row', ('col', 'depth')), may hold values from -1.5 to 1.5
- patterns: int32 [7, 32, 32], replicated, may hold values from 0 to 1, as said below
Outputs:
- sign_matrix: bfloat16 [4096, 4096], P('row', ('col', 'depth'))
Inputs may be any that keep to these rules, and one draw needn't show every extreme that they name: `patterns`: block (i, j) of every pattern is 1 where i and j are at most one apart, cyclically over 32 blocks.
All inputs are finite; a program needn't handle non-finite values.
Results may differ from a plain program's by a relative error of at most 0.0038.
The roundings to bfloat16 on the way count: a program that leaves them out, or rounds other values in their place, can miss the bound.
Values may be sent and summed in bfloat16 or wider, within the bound.
No kernel may reach another device: no remote copies, remote signals or barrier semaphores. Data moves between devices by JAX's collectives and lax.ppermute only.
A program may use at most 64 MiB of HBM per device.

v0:
```python
import functools

import jax
import jax.numpy as jnp
from jax import lax
from jax.experimental import pallas as pl
from jax.experimental.pallas import tpu as pltpu
from jax.sharding import PartitionSpec as P

BLOCK = 128
ITERS = 3
NB = 32
AXES = ("row", "col", "depth")

GROUP_CAP = 28
GROUPS = 16
CAP = 400
ZERO = GROUPS * GROUP_CAP
DUMMY = ZERO + 1
TILE = DUMMY + 1
S_BASE = TILE + 8
X_BASE = S_BASE + CAP
SLOTS = X_BASE + CAP
TERMS = 16
POSITIONS = 512
ROWS = 1152
BODY_WORDS = 24
CLASSES = ((16, 2), (8, 8), (6, 10), (5, 12), (4, 16), (3, 20), (2, 32), (1, 32), (0, 16))
STEPS = 2 * ITERS


def pack_kernel(pick_ref, in_ref, out_ref):
    for p in range(GROUP_CAP):
        out_ref[p] = in_ref[pick_ref[p]]


def product_kernel(ent_ref, ox_ref, ord_ref, body_ref, start_ref, out_ref, blocks, sem):
    for z in range(4):
        for d in range(4):
            g = z * 4 + d
            for r in range(4):
                for k in range(2):
                    pltpu.make_async_copy(
                        start_ref.at[r, z, k, d],
                        blocks.at[pl.ds(g * GROUP_CAP, GROUP_CAP), r * 2 + k],
                        sem,
                    ).start()
    blocks[ZERO] = jnp.zeros(blocks.shape[1:], blocks.dtype)
    for b in range(8):
        blocks[TILE + b] = jnp.zeros(blocks.shape[1:], blocks.dtype)
    whole = blocks.at[pl.ds(0, ZERO)]
    pltpu.make_async_copy(whole, whole, sem).wait()

    def load(slot):
        return blocks[slot].reshape(BLOCK, BLOCK)

    def step(t, carry):
        is_update = (t & 1) == 1
        keep = jnp.where(is_update, 1.5, 0.0).astype(jnp.float32)
        scale = jnp.where(is_update, -0.5, 1.0).astype(jnp.float32)
        for index, (terms, width) in enumerate(CLASSES):
            first = body_ref[t * BODY_WORDS + index * 2]
            count = body_ref[t * BODY_WORDS + index * 2 + 1]

            def body(it, carry, terms=terms, width=width, first=first):
                results = []
                for u in range(width):
                    entry = ord_ref[t * POSITIONS + first + it * width + u]
                    at = t * (TERMS * ROWS) + entry
                    words = [ent_ref[at + q * ROWS] for q in range(terms)]
                    lefts = [load(w & 0xFFFF) for w in words]
                    rights = [load(w >> 16) for w in words]
                    total = jnp.zeros((BLOCK, BLOCK), jnp.float32)
                    if terms == 1:
                        total = jnp.dot(lefts[0], rights[0], preferred_element_type=jnp.float32)
                    elif terms > 1:
                        left = jnp.concatenate(lefts, axis=1)
                        right = jnp.concatenate(rights, axis=0)
                        total = jnp.dot(left, right, preferred_element_type=jnp.float32)
                    ox = ox_ref[t * ROWS + entry]
                    old = load(ox >> 16).astype(jnp.float32)
                    results.append((ox & 0xFFFF, (keep * old + scale * total).astype(jnp.bfloat16)))
                for slot, value in results:
                    blocks[slot] = value.reshape(blocks.shape[1:])
                return carry

            lax.fori_loop(0, count, body, 0)
        return carry

    lax.fori_loop(0, STEPS, step, 0)
    copy = pltpu.make_async_copy(blocks.at[pl.ds(TILE, 8)], out_ref, sem)
    copy.start()
    copy.wait()


def ranks(mask):
    n = mask.shape[-1]
    before = (lax.iota(jnp.int32, n)[:, None] < lax.iota(jnp.int32, n)[None, :]).astype(jnp.bfloat16)
    flat = mask.reshape(-1, n).astype(jnp.bfloat16)
    return jnp.dot(flat, before, preferred_element_type=jnp.float32).astype(jnp.int32).reshape(mask.shape)


def group_order(pattern):
    return pattern.reshape(4, 8, 4, 2, 4).transpose(2, 4, 0, 3, 1).reshape(GROUPS, 64)


def fits(patterns):
    groups = group_order(patterns[0]).sum(-1).max()
    counts = patterns[1 : 2 * ITERS - 1].sum((1, 2)).max()
    f = patterns.astype(jnp.bfloat16)
    left = f[0 : 2 * ITERS].at[1::2].set(f[0 : 2 * ITERS : 2])
    right = f[0 : 2 * ITERS]
    terms = jnp.einsum("tik,tkj->tij", left, right, preferred_element_type=jnp.float32)
    most = (terms * patterns[1:].astype(jnp.float32)).max()
    return (groups <= GROUP_CAP) & (counts <= CAP) & (most <= TERMS)


def tables(patterns):
    row, col, depth = (lax.axis_index(a) for a in AXES)
    me_col = col * 4 + depth
    i = lax.iota(jnp.int32, NB)[:, None]
    j = lax.iota(jnp.int32, NB)[None, :]
    mine = (j == me_col).astype(jnp.int32)
    tile = mine * ((i // 8) == row).astype(jnp.int32)
    outs = jnp.concatenate([patterns[1:5], patterns[5:6] * mine, patterns[6:7] * tile])

    in_group = ranks(group_order(patterns[0]))
    slot0 = lax.iota(jnp.int32, GROUPS)[:, None] * GROUP_CAP + in_group
    slot0 = slot0.reshape(4, 4, 4, 2, 8).transpose(2, 4, 0, 3, 1).reshape(NB, NB)
    slot0 = jnp.where(patterns[0] > 0, slot0, ZERO)
    base = jnp.array([S_BASE, X_BASE, S_BASE, 0, S_BASE, 0], jnp.int32)[:, None]
    live = outs.reshape(STEPS, NB * NB) > 0
    out_slot = ranks(outs.reshape(STEPS, NB * NB)) + base
    in_tile = jnp.broadcast_to(TILE + i - 8 * row, (NB, NB)).reshape(1, NB * NB)
    out_slot = jnp.concatenate([out_slot[:5], in_tile])
    read_slot = jnp.where(live, out_slot, ZERO).reshape(STEPS, NB, NB)
    x_slot = jnp.stack([slot0, read_slot[1], read_slot[3]])
    left = jnp.repeat(x_slot, 2, axis=0)
    right = jnp.stack([slot0, read_slot[0], read_slot[1], read_slot[2], read_slot[3], read_slot[4]])
    old = jnp.where((lax.iota(jnp.int32, STEPS) % 2 == 1)[:, None, None], left, ZERO)

    o = lax.iota(jnp.int32, NB * NB)[None, :]
    of_row = (o // NB == i).astype(jnp.float32)
    of_col = (o % NB == i).astype(jnp.float32)
    spread = functools.partial(jnp.dot, precision=lax.Precision.HIGHEST, preferred_element_type=jnp.float32)
    wide_left = spread(left.transpose(0, 2, 1).astype(jnp.float32), of_row).astype(jnp.int32)
    wide_right = spread(right.astype(jnp.float32), of_col).astype(jnp.int32)
    on = live[:, None, :] & (wide_left != ZERO) & (wide_right != ZERO)
    before = (i > j).astype(jnp.bfloat16)
    place = jnp.einsum("kl,tlo->tko", before, on.astype(jnp.bfloat16), preferred_element_type=jnp.float32)
    blank = ZERO + ZERO * 65536
    word = jnp.where(on, wide_left + wide_right * 65536 - blank, 0)
    place = jnp.where(on, place.astype(jnp.int32), TERMS)
    hit = place[:, None] == lax.iota(jnp.int32, TERMS)[None, :, None, None]
    ent = jnp.where(hit, word[:, None], 0).sum(2) + blank
    ent = jnp.pad(ent, ((0, 0), (0, 0), (0, ROWS - NB * NB)), constant_values=blank)

    ox = out_slot + old.reshape(STEPS, NB * NB) * 65536
    ox = jnp.pad(ox, ((0, 0), (0, ROWS - NB * NB)), constant_values=DUMMY + ZERO * 65536)

    count = on.astype(jnp.int32).sum(1)
    members = []
    for (limit, _), low in zip(CLASSES, [limit for limit, _ in CLASSES[1:]] + [-1]):
        members.append(live & (count > low) & (count <= limit))
    member = jnp.stack(members, 1).astype(jnp.int32)
    rank = ranks(member)
    total = member.sum(-1)
    passed = [jnp.zeros((STEPS,), jnp.int32)]
    for index in range(len(CLASSES)):
        passed.append(passed[-1] + total[:, index])
    ahead = jnp.stack(passed[:-1], 1)
    position = jnp.where(member > 0, rank + ahead[:, :, None], 0).sum(1)
    position = jnp.where(live, position, POSITIONS)
    match = position[:, None, :] == lax.iota(jnp.int32, POSITIONS)[None, :, None]
    entry = jnp.where(match, o[None] - NB * NB, 0).sum(-1) + NB * NB
    end = jnp.zeros((STEPS,), jnp.int32)
    body = []
    for index, (_, width) in enumerate(CLASSES):
        bodies = jnp.maximum((passed[index + 1] - end + width - 1) // width, 0)
        body += [end, bodies]
        end = end + bodies * width
    body = jnp.stack(body + [end] * (BODY_WORDS - len(body)), 1)
    return ent.reshape(-1), ox.reshape(-1), entry.reshape(-1), body.reshape(-1)


def pick_places(patterns):
    _, col, depth = (lax.axis_index(a) for a in AXES)
    order = lax.dynamic_index_in_dim(group_order(patterns[0]), (col // 2) * 4 + depth, 0, keepdims=False)
    place = jnp.where(order > 0, ranks(order[None])[0], GROUP_CAP)
    hit = place[None, :] == lax.iota(jnp.int32, GROUP_CAP)[:, None]
    return jnp.where(hit, lax.iota(jnp.int32, 64)[None, :], 0).sum(-1)


def pack(pick, slices):
    return pl.pallas_call(
        pack_kernel,
        out_shape=jax.ShapeDtypeStruct((GROUP_CAP, 16, BLOCK), jnp.bfloat16),
        in_specs=[pl.BlockSpec(memory_space=pltpu.SMEM), pl.BlockSpec(memory_space=pltpu.VMEM)],
        out_specs=pl.BlockSpec(memory_space=pltpu.VMEM),
        name="pack_blocks",
    )(pick, slices)


def sparse_path(ent, ox, entry, body, start):
    smem = pl.BlockSpec(memory_space=pltpu.SMEM)
    out = pl.pallas_call(
        product_kernel,
        out_shape=jax.ShapeDtypeStruct((8, 8, 16, BLOCK), jnp.bfloat16),
        in_specs=[smem, smem, smem, smem, pl.BlockSpec(memory_space=pl.ANY)],
        out_specs=pl.BlockSpec(memory_space=pl.ANY),
        scratch_shapes=[pltpu.VMEM((SLOTS, 8, 16, BLOCK), jnp.bfloat16), pltpu.SemaphoreType.DMA(())],
        compiler_params=pltpu.CompilerParams(vmem_limit_bytes=56 * 2**20),
        name="block_products",
    )(ent, ox, entry, body, start)
    return out.reshape(8 * BLOCK, BLOCK)


def tile_mask(pattern, row_first, col_first, tile_rows, tile_cols):
    blocks = pattern.shape[0]
    slab = lax.dynamic_slice_in_dim(pattern, row_first // BLOCK, tile_rows // BLOCK, 0).astype(jnp.float32)
    col_block = (col_first + lax.iota(jnp.int32, tile_cols)) // BLOCK
    onehot = (col_block[None, :] == lax.iota(jnp.int32, blocks)[:, None]).astype(jnp.float32)
    coarse = jnp.dot(slab, onehot)
    spread_rows = jnp.broadcast_to(coarse[:, None, :], (tile_rows // BLOCK, BLOCK, tile_cols))
    return spread_rows.reshape(tile_rows, tile_cols)


def dense_path(x_in, patterns):
    tile_rows, tile_width = x_in.shape
    row_first = lax.axis_index("row") * tile_rows
    col_first = (lax.axis_index("col") * lax.axis_size("depth") + lax.axis_index("depth")) * tile_width
    masks = [tile_mask(patterns[p], row_first, col_first, tile_rows, tile_width) for p in range(2 * ITERS + 1)]
    matrix = (x_in * masks[0]).astype(jnp.bfloat16)
    for iteration in range(ITERS):
        panel = lax.all_gather(matrix, ("col", "depth"), axis=1, tiled=True)

        def product(right):
            column = lax.all_gather(right, "row", axis=0, tiled=True)
            return jnp.dot(panel, column, preferred_element_type=jnp.float32)

        squared = (masks[2 * iteration + 1] * product(matrix)).astype(jnp.bfloat16)
        update = 1.5 * matrix.astype(jnp.float32) - 0.5 * product(squared)
        matrix = (masks[2 * iteration + 2] * update).astype(jnp.bfloat16)
    return matrix


def on_device(x_in, patterns):
    groups = [[r * 8 + z * 2 + k for r in range(4) for k in range(2)] for z in range(4)]
    by_slice = x_in.reshape(8, 8, 16, BLOCK).transpose(1, 0, 2, 3)
    slices = lax.all_to_all(by_slice, ("row", "col"), 0, 0, axis_index_groups=groups, tiled=True)
    slices = slices.reshape(64, 16, BLOCK)
    packed = pack(pick_places(patterns), slices)
    start = lax.all_gather(packed, AXES, axis=0, tiled=True)
    start = start.reshape(4, 4, 2, 4, GROUP_CAP, 16, BLOCK)
    lists = tables(patterns)
    return lax.cond(
        fits(patterns),
        lambda: sparse_path(*lists, start),
        lambda: dense_path(x_in, patterns),
    )


def solution(mesh):
    placed = (P("row", ("col", "depth")), P())
    return jax.shard_map(
        on_device, mesh=mesh, in_specs=placed, out_specs=P("row", ("col", "depth")), check_vma=False
    )
```

profile of v0, /device:TPU:1, one launch (start us, length us, event | category | flops | bytes accessed | tf_op | source)
XLA Modules:
  0.0 191.2 jit_solution(1030270629373677918)
XLA Ops:
  6.5 1.7 copy.142
  8.2 5.8 %all-to-all-start = ((bf16[8,8,16,128]{3,2,1,0:T(8,128)(2,1)}), bf16[8,8,16,128]{3,2,1,0:T(8,128)(2,1)S(1)}, u32[]{:S(2)}, u32[]{:S(2)}) async-start(bf16[8,8,16,128]{3,2,1,0:T(8,128)(2,1)} %bitcast.184), calls=%async_computation | async-start | bytes 524288 | tf_op jit(solution)/shard_map/all_to_all | solution.py:250
  14.0 0.7 slice.109
  15.9 4.7 %all-to-all-done = bf16[8,8,16,128]{3,2,1,0:T(8,128)(2,1)S(1)} async-done(((bf16[8,8,16,128]{3,2,1,0:T(8,128)(2,1)}), bf16[8,8,16,128]{3,2,1,0:T(8,128)(2,1)S(1)}, u32[]{:S(2)}, u32[]{:S(2)}) %all-to-all-start) | async-done | bytes 262176 | tf_op jit(solution)/shard_map/all_to_all | solution.py:250
  20.5 0.7 copy-done.3
  21.2 1.6 pack_blocks.1
  23.4 0.8 slice_multiply_fusion
  24.2 1.0 fusion.110
  25.5 0.9 convert_element_type.186
  27.1 0.7 fusion.75
  28.9 0.7 convert_reduce_fusion
  33.1 0.7 reduce_max.28
  34.5 0.8 fusion.65
  37.4 0.7 stack.14
  38.7 62.7 %all-gather.29.cloned.1.call-done = bf16[3584,16,128]{2,1,0:T(8,128)(2,1)} async-done(((bf16[28,16,128]{2,1,0:T(8,128)(2,1)}), bf16[3584,16,128]{2,1,0:T(8,128)(2,1)}) %all-gather.29.cloned.1.call-update) | async-done | bytes 14680080 | tf_op jit(solution)/shard_map/all_gather | solution.py:253
  101.5 6.1 %eq.85 = s32[6,16,32,1024]{3,2,1,0:T(8,128)} iota(), iota_dimension=1 | iota | bytes 12582912 | tf_op jit(solution)/shard_map/eq | solution.py:154
  107.6 5.8 %eq.86 = s32[6,512,1024]{2,1,0:T(8,128)} iota(), iota_dimension=1 | iota | bytes 12582912 | tf_op jit(solution)/shard_map/eq | solution.py:174
  115.2 68.4 %conditional.1 = (bf16[1024,128]{1,0:T(8,128)(2,1)S(1)}) conditional(s32[]{:T(128)} %convert_element_type.188, (s32[7,32,32]{2,1,0:T(8,128)S(1)}, bf16[1024,128]{1,0:T(8,128)(2,1)S(1)}) %tuple.258, (pred[6,32,1024]{2,1,0:T(32,128)(4,1)S(1)}, s32[6,32,1024]{2,1,0:T(8,128)S(1)}, s32[6,16,32,1024]{3,2,1,0:T(8,128)}, s32[6,32,1024]{2,1,0:T(8,128)S(1)}, ...), branch_computations={%region_9.10_spmd, %region_10.14_spmd} | conditional | flops 6446481408 | bytes 170541824 | solution.py:256
  115.5 7.6 %select_reduce_fusion.1 = s32[6,16,1024]{2,1,0:T(8,128)S(1)} fusion(s32[6,16,32,1024]{3,2,1,0:T(8,128)} %get-tuple-element.141, s32[6,32,1024]{2,1,0:T(8,128)S(1)} %get-tuple-element.286, s32[6,32,1024]{2,1,0:T(8,128)S(1)} %get-tuple-element.285), kind=kLoop, calls=%fused_computation.69 | loop fusion | flops 9338880 | bytes 14548992 | tf_op jit(solution)/shard_map/reduce_sum | solution.py:155
  123.2 0.8 reshape.544.ent_ref
  124.5 5.9 %select_reduce_fusion = s32[6,512]{1,0:T(8,128)S(1)} fusion(s32[6,512,1024]{2,1,0:T(8,128)} %get-tuple-element.152, s32[1024]{0:T(1024)S(1)} %bitcast.200, s32[6,1024]{1,0:T(8,128)S(1)} %bitcast.199), kind=kLoop, calls=%fused_computation.68 | loop fusion | flops 9434112 | bytes 12623872 | tf_op jit(solution)/shard_map/reduce_sum | solution.py:175
  131.8 0.7 reshape.548.body_ref
  132.5 51.1 %block_products.1 = bf16[8,8,16,128]{3,2,1,0:T(8,128)(2,1)S(1)} custom-call(s32[110592]{0:T(1024)} %reshape.544.ent_ref, s32[6912]{0:T(1024)} %reshape.546.ox_ref, s32[3072]{0:T(1024)} %add.667.ord_ref, s32[144]{0:T(256)} %reshape.548.body_ref, bf16[4,4,2,4,28,16,128]{6,5,4,3,2,1,0:T(8,128)(2,1)} %bitcast.187), custom_call_target="tpu_custom_call" | custom-call | tf_op jit(solution)/shard_map/cond/branch_1_fun/block_products/pallas_call | solution.py:206
  183.7 0.7 copy-done.9
  (120 shorter events, 12.1 us)
Async XLA Ops:
  6.5 27.9 %copy-start.1 = (s32[7,32,32]{2,1,0:T(8,128)S(1)}, s32[7,32,32]{2,1,0:T(8,128)}, u32[]{:S(2)}) copy-start(s32[7,32,32]{2,1,0:T(8,128)} %param.6) | copy-start | bytes 86020
  8.2 12.3 %all-to-all-start = ((bf16[8,8,16,128]{3,2,1,0:T(8,128)(2,1)}), bf16[8,8,16,128]{3,2,1,0:T(8,128)(2,1)S(1)}, u32[]{:S(2)}, u32[]{:S(2)}) async-start(bf16[8,8,16,128]{3,2,1,0:T(8,128)(2,1)} %bitcast.184), calls=%async_computation | async-start | bytes 524288 | tf_op jit(solution)/shard_map/all_to_all | solution.py:250
  14.0 87.4 %all-gather.29.cloned.1.call-start = ((), (), s32[]{:S(2)}) async-start(), calls=%async_computation.10 | async-start | bytes 14794752 | tf_op jit(solution)/shard_map/all_gather | solution.py:253
  20.5 0.7 copy-start.3
  107.6 7.6 %copy-start.2 = (bf16[1024,128]{1,0:T(8,128)(2,1)S(1)}, bf16[1024,128]{1,0:T(8,128)(2,1)}, u32[]{:S(2)}) copy-start(bf16[1024,128]{1,0:T(8,128)(2,1)} %param.5) | copy-start | bytes 786436
  115.5 9.0 %copy-start.8 = (s32[1,1,1024]{2,1,0:T(1,128)S(1)}, s32[1,1,1024]{2,1,0:T(1,128)}, u32[]{:S(2)}) copy-start(s32[1,1,1024]{2,1,0:T(1,128)} %get-tuple-element.153) | copy-start | bytes 12292 | tf_op jit(solution)/shard_map/cond
  123.1 8.0 %copy-start.10 = (s32[6,1,1]{0,2,1:T(1,128)S(1)}, s32[6,1,1]{0,2,1:T(1,128)}, u32[]{:S(2)}) copy-start(s32[6,1,1]{0,2,1:T(1,128)} %get-tuple-element.145) | copy-start | bytes 76 | tf_op jit(solution)/shard_map/cond
  123.1 8.1 %copy-start.6 = (s32[6,1024]{1,0:T(8,128)S(1)}, s32[6,1024]{1,0:T(8,128)}, u32[]{:S(2)}) copy-start(s32[6,1024]{1,0:T(8,128)} %get-tuple-element.147) | copy-start | bytes 73732 | tf_op jit(solution)/shard_map/cond
  123.1 8.7 %copy-start.7 = (s32[6,24]{1,0:T(8,128)S(1)}, s32[6,24]{1,0:T(8,128)}, u32[]{:S(2)}) copy-start(s32[6,24]{1,0:T(8,128)} %get-tuple-element.154) | copy-start | bytes 1732 | tf_op jit(solution)/shard_map/cond
  183.7 0.7 copy-start.9
Sparse Core Ops, SparseCore 0:
  23.0 78.3 all-gather.28
where the time goes:
time: 194 us; the launch traced here: 191 us
  waiting for transfers between devices  67.4 us (35%)
  Pallas kernels  52.8 us (27%)
  local copies, waits for them, and re-layouts  25.5 us (13%)
  other arithmetic  20.7 us (11%)
  between operations  15.8 us (8%)
  starting transfers between devices  5.8 us (3%)
  matrix products  3.15 us (2%)
    all_gather x1, waiting for transfers between devices, on_device(): start = lax.all_gather(packed, AXES, axis=0, tiled=True)  62.7 us
    pallas_call x1, Pallas kernels, sparse_path(): pl.pallas_call(product_kernel, out_shape=jax.ShapeDtypeStruct((8, 8, 16,...  51.1 us
    reduce_sum x1, other arithmetic, tables(): ent = jnp.where(hit, word[:, None], 0).sum(2) + blank  7.56 us
    eq x1, local copies, waits for them, and re-layouts, tables(): hit = place[:, None] == lax.iota(jnp.int32, TERMS)[None, :, None, None]  6.15 us
    reduce_sum x1, other arithmetic, tables(): entry = jnp.where(match, o[None] - NB * NB, 0).sum(-1) + NB * NB  5.91 us
    eq x1, local copies, waits for them, and re-layouts, tables(): position[:, None, :] == lax.iota(jnp.int32, POSITIONS)[None, :, None]  5.84 us
    all_to_all x1, starting transfers between devices, on_device(): lax.all_to_all(by_slice, ('row', 'col'), 0, 0, axis_index_groups=groups,...  5.8 us
    all_to_all x1, waiting for transfers between devices, on_device(): lax.all_to_all(by_slice, ('row', 'col'), 0, 0, axis_index_groups=groups,...  4.67 us
  transfers between devices with their start and end apart: 2, of which 2 were waited for; matrix products, arithmetic and copies ran while one was open for 8% of the time, Pallas kernels for 0%

commit v1 on v0

--- a/solution.py
+++ b/solution.py
@@ -252,7 +252,7 @@
     packed = pack(pick_places(patterns), slices)
     start = lax.all_gather(packed, AXES, axis=0, tiled=True)
     start = start.reshape(4, 4, 2, 4, GROUP_CAP, 16, BLOCK)
-    lists = tables(patterns)
+    lists = lax.optimization_barrier(tables(patterns))
     return lax.cond(
         fits(patterns),
         lambda: sparse_path(*lists, start),

time: 194 us -> 168 us (0.87); the launches traced: 191 us -> 170 us
  local copies, waits for them, and re-layouts: 25.5 us -> 8.38 us
  Pallas kernels: 52.8 us -> 62.7 us
  other arithmetic: 20.7 us -> 11.4 us
  waiting for transfers between devices: 67.4 us -> 62.7 us
    eq x2 -> x0, local copies, waits for them, and re-layouts: 12 us -> none  [the longest x1 6.15 us: tables(): hit = place[:, None] == lax.iota(jnp.int32, TERMS)[None, :, None, None]]
    pallas_call x1, Pallas kernels: 51.1 us -> 61.1 us  [sparse_path(): pl.pallas_call(product_kernel, out_shape=jax.ShapeDtypeStruct((8, 8, 16,...]
    reduce_sum x1, other arithmetic: 7.56 us -> 2.56 us  [tables(): ent = jnp.where(hit, word[:, None], 0).sum(2) + blank]
    all_gather x1, waiting for transfers between devices: 62.7 us -> 58.1 us  [on_device(): start = lax.all_gather(packed, AXES, axis=0, tiled=True)]
    reduce_sum x1, other arithmetic: 5.91 us -> 1.54 us  [tables(): entry = jnp.where(match, o[None] - NB * NB, 0).sum(-1) + NB * NB]
  transfers between devices with their start and end apart: 2 -> 2, of which waited for: 2 -> 2; matrix products, arithmetic and copies ran while one was open for 8% -> 12% of each run, Pallas kernels for 0% -> 0%
where the time goes in v1:
time: 168 us; the launch traced here: 170 us
  waiting for transfers between devices  62.7 us (37%)
  Pallas kernels  62.7 us (37%)
  between operations  15.7 us (9%)
  other arithmetic  11.4 us (7%)
  local copies, waits for them, and re-layouts  8.38 us (5%)
  starting transfers between devices  5.8 us (3%)
  matrix products  3.4 us (2%)
    pallas_call x1, Pallas kernels, sparse_path(): pl.pallas_call(product_kernel, out_shape=jax.ShapeDtypeStruct((8, 8, 16,...  61.1 us
    all_gather x1, waiting for transfers between devices, on_device(): start = lax.all_gather(packed, AXES, axis=0, tiled=True)  58.1 us
    all_to_all x1, starting transfers between devices, on_device(): lax.all_to_all(by_slice, ('row', 'col'), 0, 0, axis_index_groups=groups,...  5.8 us
    all_to_all x1, waiting for transfers between devices, on_device(): lax.all_to_all(by_slice, ('row', 'col'), 0, 0, axis_index_groups=groups,...  4.58 us
  transfers between devices with their start and end apart: 2, of which 2 were waited for; matrix products, arithmetic and copies ran while one was open for 12% of the time, Pallas kernels for 0%

profile of v1, /device:TPU:1, one launch (start us, length us, event | category | flops | bytes accessed | tf_op | source)
XLA Modules:
  0.0 170.1 jit_solution(516311006643475306)
XLA Ops:
  6.5 1.7 copy.127
  8.2 5.8 %all-to-all-start = ((bf16[8,8,16,128]{3,2,1,0:T(8,128)(2,1)}), bf16[8,8,16,128]{3,2,1,0:T(8,128)(2,1)S(1)}, u32[]{:S(2)}, u32[]{:S(2)}) async-start(bf16[8,8,16,128]{3,2,1,0:T(8,128)(2,1)} %bitcast.181), calls=%async_computation | async-start | bytes 524288 | tf_op jit(solution)/shard_map/all_to_all | solution.py:250
  14.0 0.7 slice.109
  15.2 0.7 select_reduce_fusion.2.pick_ref
  15.9 4.6 %all-to-all-done = bf16[8,8,16,128]{3,2,1,0:T(8,128)(2,1)S(1)} async-done(((bf16[8,8,16,128]{3,2,1,0:T(8,128)(2,1)}), bf16[8,8,16,128]{3,2,1,0:T(8,128)(2,1)S(1)}, u32[]{:S(2)}, u32[]{:S(2)}) %all-to-all-start) | async-done | bytes 262176 | tf_op jit(solution)/shard_map/all_to_all | solution.py:250
  20.5 0.7 copy-done.3
  21.2 1.6 pack_blocks.1
  23.3 0.8 constant_dynamic-update-slice_fusion.5
  24.2 1.0 fusion.120
  25.5 0.9 convert_element_type.186
  27.0 0.7 fusion.82
  28.4 0.6 fusion.71
  28.9 0.6 fusion.72
  33.2 1.5 select_reduce_fusion
  34.8 0.6 fusion.58
  35.4 2.6 %select_reduce_fusion.1 = s32[6,16,1024]{2,1,0:T(8,128)S(1)} fusion(s32[6,32,1024]{2,1,0:T(8,128)S(1)} %get-tuple-element.84, s32[6,32,1024]{2,1,0:T(8,128)S(1)} %fusion.58), kind=kLoop, calls=%fused_computation.70 | loop fusion | flops 9338880 | bytes 1966080 | tf_op jit(solution)/shard_map/reduce_sum | solution.py:155
  38.7 0.6 reduce_max.27
  39.3 0.7 reduce_max.28
  40.0 0.6 scatter_fusion
  40.7 0.8 fusion.68
  43.3 58.1 %all-gather.29.cloned.1.call-done = bf16[3584,16,128]{2,1,0:T(8,128)(2,1)} async-done(((bf16[28,16,128]{2,1,0:T(8,128)(2,1)}), bf16[3584,16,128]{2,1,0:T(8,128)(2,1)}) %all-gather.29.cloned.1.call-update) | async-done | bytes 14680080 | tf_op jit(solution)/shard_map/all_gather | solution.py:253
  101.4 61.1 %conditional.1 = (bf16[1024,128]{1,0:T(8,128)(2,1)S(1)}) conditional(s32[]{:T(128)} %convert_element_type.188, (s32[7,32,32]{2,1,0:T(8,128)S(1)}, bf16[1024,128]{1,0:T(8,128)(2,1)S(1)}) %tuple.84, (bf16[3584,16,128]{2,1,0:T(8,128)(2,1)}, s32[110592]{0:T(1024)S(1)}, s32[6912]{0:T(1024)S(1)}, s32[3072]{0:T(1024)S(1)}, s32[144]{0:T(256)S(1)}) %tuple.14), branch_computations={%region_12.13_spmd, %region_13.14_spmd} | conditional | flops 6446481408 | bytes 170541824 | solution.py:256
  101.4 61.1 %block_products.1 = bf16[8,8,16,128]{3,2,1,0:T(8,128)(2,1)S(1)} custom-call(s32[110592]{0:T(1024)S(1)} %get-tuple-element.25.ent_ref, s32[6912]{0:T(1024)S(1)} %get-tuple-element.26.ox_ref, s32[3072]{0:T(1024)S(1)} %get-tuple-element.27.ord_ref, s32[144]{0:T(256)S(1)} %get-tuple-element.28.body_ref, bf16[4,4,2,4,28,16,128]{6,5,4,3,2,1,0:T(8,128)(2,1)} %bitcast.184), custom_call_target="tpu_custom_call" | custom-call | tf_op jit(solution)/shard_map/cond/branch_1_fun/block_products/pallas_call | solution.py:206
  162.5 0.7 copy-done.6
  (105 shorter events, 6.7 us)
Async XLA Ops:
  8.2 12.3 %all-to-all-start = ((bf16[8,8,16,128]{3,2,1,0:T(8,128)(2,1)}), bf16[8,8,16,128]{3,2,1,0:T(8,128)(2,1)S(1)}, u32[]{:S(2)}, u32[]{:S(2)}) async-start(bf16[8,8,16,128]{3,2,1,0:T(8,128)(2,1)} %bitcast.181), calls=%async_computation | async-start | bytes 524288 | tf_op jit(solution)/shard_map/all_to_all | solution.py:250
  14.0 87.4 %all-gather.29.cloned.1.call-start = ((), (), s32[]{:S(2)}) async-start(), calls=%async_computation.10 | async-start | bytes 14794752 | tf_op jit(solution)/shard_map/all_gather | solution.py:253
  20.5 0.7 copy-start.3
  28.9 11.7 %copy-start.1 = (s32[7,32,32]{2,1,0:T(8,128)S(1)}, s32[7,32,32]{2,1,0:T(8,128)}, u32[]{:S(2)}) copy-start(s32[7,32,32]{2,1,0:T(8,128)} %param.6) | copy-start | bytes 86020
  28.9 72.5 %copy-start.2 = (bf16[1024,128]{1,0:T(8,128)(2,1)S(1)}, bf16[1024,128]{1,0:T(8,128)(2,1)}, u32[]{:S(2)}) copy-start(bf16[1024,128]{1,0:T(8,128)(2,1)} %param.5) | copy-start | bytes 786436
  162.5 0.7 copy-start.6
Sparse Core Ops, SparseCore 0:
  23.0 78.4 all-gather.28
